TPU v7x, 256 devices: a whole 4x4x8 slice. The times are simulated.
256 devices in a mesh: seed: 4 (over x), fsdp: 8 (over y, core), seq: 8 (over z).
Axes of the slice: x: 4, y: 4, z: 8, core: 2. Of those that a mesh axis runs over, the one named last changes fastest.
Arguments:
- mel_frames: bfloat16 [8, 32768, 80], P('fsdp', 'seq'), may hold values from -6 to 6
- lengths: int32 [8], P('fsdp'), may hold values from 1 to 8192, 40960 in all
- targets: int32 [8, 8192], P('fsdp', 'seq'), may hold values from 0 to 511
- frame_mask: int32 [8, 8192], P('fsdp', 'seq'), may hold values 0 or 1
- stem_weight: bfloat16 [4, 640, 1536], P('seed'), may hold values from -0.25 to 0.25
- conv_in_weight: bfloat16 [4, 1536, 1536], P('seed', ('fsdp', 'seq')), may hold values from -0.15625 to 0.15625
- conv_out_weight: bfloat16 [4, 768, 1536], P('seed', ('fsdp', 'seq')), may hold values from -0.21875 to 0.21875
- depth_weight: bfloat16 [4, 31, 768], P('seed'), may hold values from -1 to 1
- head_weight: bfloat16 [4, 1536, 512], P('seed', ('fsdp', 'seq')), may hold values from -80 to 80
- norm_gain: float32 [4, 2, 1536], P('seed'), may hold values from 0.5 to 1.5
Outputs:
- frame_error: float32 [8, 8192], P('fsdp', 'seq')
- utt_score: float32 [8], P('fsdp')
Inputs may be any that keep to these rules, and one draw needn't show every extreme that they name: `lengths`: some utterance has exactly 8192 valid frames.
All inputs are finite; a program needn't handle non-finite values. No bound on the sum of `lengths` or of `frame_mask` on one device may be relied on, other than what follows from the above.
Results may differ from a plain program's by a relative error of at most 0.0022.
Values may be sent and summed in bfloat16 or wider, within the bound.
A program may use at most 64 MiB of HBM per device.

v0:
```python
import jax
import jax.numpy as jnp
from jax import lax
from jax.sharding import PartitionSpec as P


def from_behind(x, axis, by):
    count = lax.axis_size(axis)
    pairs = [(i, i + by) for i in range(count) if 0 <= i + by < count]
    return lax.ppermute(x, axis, pairs)


def extended(x, sides, width):
    for axis, dim in sides:
        count, length = (lax.axis_size(axis), x.shape[dim])
        up = [(i, (i + 1) % count) for i in range(count - 1)]
        down = [(j, i) for i, j in up]
        last = lax.slice_in_dim(x, length - width, length, axis=dim)
        first = lax.slice_in_dim(x, 0, width, axis=dim)
        before = lax.ppermute(last, axis, up)
        after = lax.ppermute(first, axis, down)
        x = jnp.concatenate([before, x, after], axis=dim)
    return x


def layer_norm(values, gain_row):
    row_mean = jnp.mean(values, axis=-1, keepdims=True)
    centred = values - row_mean
    row_var = jnp.mean(centred * centred, axis=-1, keepdims=True)
    return (centred * lax.rsqrt(row_var + 1e-05) * gain_row).astype(jnp.bfloat16)


def block_product(left_rows, right_matrix):
    return jnp.dot(left_rows, right_matrix, preferred_element_type=jnp.float32)


def row_product(activations, shard_piece):
    return block_product(activations, shard_piece[0])


def body(
    mel_frames,
    lengths,
    targets,
    frame_mask,
    stem_weight,
    conv_in_weight,
    conv_out_weight,
    depth_weight,
    head_weight,
    norm_gain,
):
    frame_rows = targets.shape[1]
    blocks = mel_frames[0].reshape(frame_rows, -1)
    next_block = from_behind(blocks[:1], "seq", -1)
    following = jnp.concatenate([blocks[1:], next_block], 0)
    half_width = blocks.shape[1]
    stem_matrix = stem_weight[0]
    stem_out = (
        jnp.dot(blocks, stem_matrix[:half_width], preferred_element_type=jnp.float32)
        + jnp.dot(following, stem_matrix[half_width:], preferred_element_type=jnp.float32)
    ).astype(jnp.bfloat16)
    offset = lax.axis_index("seq") * frame_rows
    length = lengths[0]
    positions = offset + jnp.arange(frame_rows, dtype=jnp.int32)
    frame_live = positions < length
    gain_rows = norm_gain[0]
    normed_one = layer_norm(stem_out.astype(jnp.float32), gain_rows[0])
    tap_count = depth_weight.shape[1]
    channels = depth_weight.shape[2]
    halo_width = tap_count // 2
    mixed_rows = row_product(
        normed_one, lax.all_gather(conv_in_weight, ("fsdp", "seq"), axis=1, tiled=True)
    )
    input_positions = offset + jnp.arange(normed_one.shape[0], dtype=jnp.int32)
    input_live = jnp.logical_and(input_positions >= 0, input_positions < length)
    gated_rows = (
        mixed_rows[:, :channels]
        * jax.nn.sigmoid(mixed_rows[:, channels:])
        * input_live[:, None].astype(jnp.float32)
    ).astype(jnp.bfloat16)
    padded = extended(gated_rows, (("seq", 0),), halo_width)
    depthwise = jnp.zeros((frame_rows, channels), jnp.float32)
    for tap_index in range(tap_count):
        depthwise = depthwise + padded[tap_index : tap_index + frame_rows].astype(
            jnp.float32
        ) * depth_weight[0, tap_index].astype(jnp.float32)
    swished = jax.nn.silu(depthwise).astype(jnp.bfloat16)
    conv_proj = row_product(
        swished, lax.all_gather(conv_out_weight, ("fsdp", "seq"), axis=1, tiled=True)
    )
    after_conv = stem_out.astype(jnp.float32) + conv_proj
    normed_two = layer_norm(after_conv, gain_rows[1])
    logits = row_product(
        normed_two, lax.all_gather(head_weight, ("fsdp", "seq"), axis=1, tiled=True)
    )
    posterior = jax.nn.softmax(logits, axis=-1)
    vocab_size = logits.shape[1]
    onehot = (jnp.arange(vocab_size, dtype=jnp.int32)[None, :] == targets[0][:, None]).astype(
        jnp.float32
    )
    differ = posterior - onehot
    frame_err = (
        jnp.sqrt(jnp.sum(differ * differ, axis=-1))
        * frame_live.astype(jnp.float32)
        * frame_mask[0].astype(jnp.float32)
    )
    seed_count = lax.axis_size("seed")
    frame_error = lax.psum(frame_err, "seed") / jnp.float32(seed_count)
    numerator = lax.psum(jnp.sum(frame_error), "seq")
    utt_score = numerator / length.astype(jnp.float32)
    return (frame_error[None, :], utt_score.reshape(1))


def solution(mesh):
    in_specs = (
        P("fsdp", "seq", None),
        P("fsdp"),
        P("fsdp", "seq"),
        P("fsdp", "seq"),
        P("seed", None, None),
        P("seed", ("fsdp", "seq"), None),
        P("seed", ("fsdp", "seq"), None),
        P("seed", None, None),
        P("seed", ("fsdp", "seq"), None),
        P("seed", None, None),
    )
    out_specs = (P("fsdp", "seq"), P("fsdp"))
    return jax.shard_map(body, mesh=mesh, in_specs=in_specs, out_specs=out_specs, check_vma=False)
```

profile of v0, /device:TPU:8, one launch (start us, length us, event | category | flops | bytes accessed | tf_op | source)
XLA Modules:
  0.0 291.0 jit_solution(8486558325888110013)
XLA Ops:
  7.2 0.0 copy-start.3
  7.2 0.0 all-gather.4.cloned.1.call-start
  7.2 0.7 all-gather.4.cloned.1.call-update
  7.9 0.0 all-gather.6.cloned.1.call-start
  8.0 1.5 copy.22
  9.4 0.0 all-gather.6.cloned.1.call-update
  9.5 0.0 all-gather.8.cloned.1.call-start
  9.5 0.7 slice.261
  10.2 0.1 copy.21
  10.3 0.1 slice.262
  10.4 1.3 collective-permute-start
  11.7 0.0 all-gather.8.cloned.1.call-update
  11.7 1.6 copy.19
  13.3 1.4 convert_reduce_fusion.31
  14.8 0.7 reshape_squeeze.3
  15.4 0.0 copy-done.3
  16.1 0.0 copy-start
  16.2 5.7 %fusion.54 = f32[1024,1536]{1,0:T(8,128)} fusion(bf16[1024,320]{1,0:T(8,128)(2,1)S(1)} %reshape_squeeze.3, bf16[1,640,1536]{2,1,0:T(8,128)(2,1)} %param.14), kind=kOutput, calls=%fused_computation.110 | convolution fusion | flops 1006632960 | bytes 7929856 | tf_op jit(solution)/shard_map/dot_general | solution.py:60
  21.9 0.0 copy-done
  21.9 0.2 slice.259
  22.1 0.6 copy.20
  22.8 1.6 slice.260
  24.4 0.0 collective-permute-done
  24.4 5.3 %convert_reduce_fusion = (f32[1024]{0:T(1024)S(1)}, bf16[1024,1536]{1,0:T(8,128)(2,1)S(1)}) fusion(f32[1024,1536]{1,0:T(8,128)} %fusion.54, bf16[1,640,1536]{2,1,0:T(8,128)(2,1)} %param.14, bf16[1,320]{1,0:T(2,128)(2,1)S(1)} %collective-permute-done, bf16[1023,320]{1,0:T(8,128)(2,1)} %slice.260), kind=kOutput, calls=%fused_computation.2 | convolution fusion | flops 1014234112 | bytes 11211392 | tf_op jit(solution)/shard_map/dot_general | solution.py:61
  29.7 1.0 fusion.2
  30.7 61.1 %all-gather.4.cloned.1.call-done = bf16[1,1536,1536]{2,1,0:T(8,128)(2,1)} async-done(((bf16[1,24,1536]{2,1,0:T(8,128)(2,1)}), bf16[1,1536,1536]{2,1,0:T(8,128)(2,1)}) %all-gather.4.cloned.1.call-update) | async-done | bytes 4718608 | tf_op jit(solution)/shard_map/all_gather | solution.py:73
  91.7 7.2 %fusion.5 = f32[1024,1536]{1,0:T(8,128)S(1)} fusion(bf16[1,1536,1536]{2,1,0:T(8,128)(2,1)} %all-gather.4.cloned.1.call-done, bf16[1024,1536]{1,0:T(8,128)(2,1)S(1)} %get-tuple-element.40, f32[1536]{0:T(1024)S(1)} %get-tuple-element.34, f32[1024]{0:T(1024)S(1)} %add_rsqrt_fusion.1, f32[1024]{0:T(1024)S(1)} %broadcast_multiply_fusion.2), kind=kOutput, calls=%fused_computation.39 | convolution fusion | flops 4839702528 | bytes 14170112 | tf_op jit(solution)/shard_map/dot_general | solution.py:34
  99.0 0.0 copy-start.2
  99.0 0.0 copy-start.5
  99.0 0.8 fusion.20
  99.9 0.0 copy-start.1
  99.9 1.1 copy-done.1
  101.0 3.1 %collective-permute-start.1 = (bf16[15,768]{1,0:T(8,128)(2,1)S(1)}, bf16[15,768]{1,0:T(8,128)(2,1)S(1)}, u32[]{:S(2)}, u32[]{:S(2)}) collective-permute-start(bf16[15,768]{1,0:T(8,128)(2,1)S(1)} %get-tuple-element.35), channel_id=1, source_target_pairs={{0,1},{1,2},{2,3},{3,4},{4,5},{5,6},{6,7},{8,9},{9,10},{10,11},{11... | collective-permute-start | bytes 69128 | tf_op jit(solution)/shard_map/ppermute | solution.py:20
  104.1 1.5 collective-permute-start.2
  105.6 0.0 copy-done.2
  105.6 0.1 convert_reduce_fusion.30
  105.7 0.0 copy-done.5
  105.8 65.5 %all-gather.6.cloned.1.call-done = bf16[1,768,1536]{2,0,1:T(2,128)(2,1)} async-done(((bf16[1,12,1536]{2,0,1:T(2,128)(2,1)}), bf16[1,768,1536]{2,0,1:T(2,128)(2,1)}) %all-gather.6.cloned.1.call-update) | async-done | bytes 2359312 | tf_op jit(solution)/shard_map/all_gather | solution.py:90
  171.3 0.0 collective-permute-done.1
  171.3 0.0 collective-permute-done.2
  171.3 48.2 %fusion.70 = (f32[1024]{0:T(1024)S(1)}, f32[1024,1536]{1,0:T(8,128)}) fusion(bf16[1,768,1536]{2,0,1:T(2,128)(2,1)} %all-gather.6.cloned.1.call-done, bf16[1024,768]{1,0:T(8,128)(2,1)} %copy-done.1, bf16[15,768]{1,0:T(8,128)(2,1)S(1)} %collective-permute-done.2, bf16[15,768]{1,0:T(8,128)(2,1)S(1)} %collective-permute-done.1, ...), kind=kOutput, calls=%fused_computation.166 | convolution fusion | flops 2567699456 | bytes 13514752 | tf_op jit(solution)/shard_map/dot_general | solution.py:34
  219.5 3.6 %multiply_reduce_fusion = f32[1024]{0:T(1024)S(1)} fusion(f32[1024,1536]{1,0:T(8,128)} %get-tuple-element.42, f32[1024]{0:T(1024)S(1)} %broadcast_multiply_fusion.1), kind=kLoop, calls=%fused_computation.37 | loop fusion | flops 4717568 | bytes 6299648 | tf_op jit(solution)/shard_map/reduce_sum | solution.py:29
  223.1 25.5 %all-gather.8.cloned.1.call-done = bf16[1,1536,512]{2,1,0:T(8,128)(2,1)} async-done(((bf16[1,24,512]{2,1,0:T(8,128)(2,1)}), bf16[1,1536,512]{2,1,0:T(8,128)(2,1)}) %all-gather.8.cloned.1.call-update) | async-done | bytes 1572880 | tf_op jit(solution)/shard_map/all_gather | solution.py:95
  248.6 0.0 copy-start.4
  248.6 5.0 %fusion.71 = (f32[1024]{0:T(1024)S(1)}, f32[1024,512]{0,1:T(8,128)S(1)}) fusion(bf16[1,1536,512]{2,1,0:T(8,128)(2,1)} %all-gather.8.cloned.1.call-done, f32[1024,1536]{1,0:T(8,128)} %get-tuple-element.42, f32[1536]{0:T(1024)S(1)} %get-tuple-element.33, f32[1024]{0:T(1024)S(1)} %add_rsqrt_fusion, f32[1024]{0:T(1024)S(1)} %broadcast_multiply_fusion.1), kind=kOutput, calls=%fused_computation.167 | convolution fusion | flops 1617427456 | bytes 9979904 | tf_op jit(solution)/shard_map/dot_general | solution.py:34
  253.6 0.3 fusion.23
  254.0 0.0 copy-done.4
  254.0 0.7 multiply_reduce_fusion.1
  254.7 10.4 %psum.14 = f32[1024]{0:T(1024)S(1)} all-reduce(f32[1024]{0:T(1024)S(1)} %select_multiply_fusion), channel_id=1, replica_groups=mesh['seed'=4,'fsdp'=8,'seq'=8] {'seed'}, use_global_device_ids=true, to_apply=%region_7.8 | all-reduce | flops 1024 | bytes 8192 | tf_op jit(solution)/shard_map/psum | solution.py:109
  265.1 1.2 fusion.68
  266.3 16.4 %psum.15 = f32[]{:T(128)} all-reduce(f32[]{:T(128)} %get-tuple-element.37), channel_id=1, replica_groups=mesh['seed'=4,'fsdp'=8,'seq'=8] {'seq'}, use_global_device_ids=true, to_apply=%region_9.10 | all-reduce | flops 1 | bytes 8 | tf_op jit(solution)/shard_map/psum | solution.py:110
  (9 shorter events, 0.1 us)
Async XLA Ops:
  7.2 8.3 %copy-start.3 = (f32[1,2,1536]{2,1,0:T(2,128)S(1)}, f32[1,2,1536]{2,1,0:T(2,128)}, u32[]{:S(2)}) copy-start(f32[1,2,1536]{2,1,0:T(2,128)} %param.19) | copy-start | bytes 36868
  7.2 84.6 %all-gather.4.cloned.1.call-start = ((), (), s32[]{:S(2)}) async-start(), calls=%async_computation | async-start | bytes 4792320 | tf_op jit(solution)/shard_map/all_gather | solution.py:73
  7.9 163.4 %all-gather.6.cloned.1.call-start = ((), (), s32[]{:S(2)}) async-start(), calls=%async_computation.1 | async-start | bytes 4792320 | tf_op jit(solution)/shard_map/all_gather | solution.py:90
  9.5 239.1 %all-gather.8.cloned.1.call-start = ((), (), s32[]{:S(2)}) async-start(), calls=%async_computation.2 | async-start | bytes 1597440 | tf_op jit(solution)/shard_map/all_gather | solution.py:95
  10.4 14.0 %collective-permute-start = (bf16[1,320]{1,0:T(2,128)(2,1)S(1)}, bf16[1,320]{1,0:T(2,128)(2,1)S(1)}, u32[]{:S(2)}, u32[]{:S(2)}) collective-permute-start(bf16[1,320]{1,0:T(2,128)(2,1)S(1)} %slice.262), channel_id=1, source_target_pairs={{1,0},{2,1},{3,2},{4,3},{5,4},{6,5},{7,6},{9,8},{10,9},{11,10},{12... | collective-permute-start | bytes 1928 | tf_op jit(solution)/shard_map/ppermute | solution.py:10
  16.1 5.7 %copy-start = (bf16[1,4096,80]{1,2,0:T(8,128)(2,1)S(1)}, bf16[1,4096,80]{1,2,0:T(8,128)(2,1)}, u32[]{:S(2)}) copy-start(bf16[1,4096,80]{1,2,0:T(8,128)(2,1)} %param.10) | copy-start | bytes 1966084
  99.0 6.6 %copy-start.2 = (bf16[1,31,768]{2,1,0:T(8,128)(2,1)S(1)}, bf16[1,31,768]{2,1,0:T(8,128)(2,1)}, u32[]{:S(2)}) copy-start(bf16[1,31,768]{2,1,0:T(8,128)(2,1)} %param.17) | copy-start | bytes 142852
  99.0 6.7 %copy-start.5 = (s32[1,1024]{1,0:T(1,128)S(1)}, s32[1,1024]{1,0:T(1,128)}, u32[]{:S(2)}) copy-start(s32[1,1024]{1,0:T(1,128)} %param.13) | copy-start | bytes 12292
  99.9 1.1 copy-start.1
  101.0 70.3 %collective-permute-start.1 = (bf16[15,768]{1,0:T(8,128)(2,1)S(1)}, bf16[15,768]{1,0:T(8,128)(2,1)S(1)}, u32[]{:S(2)}, u32[]{:S(2)}) collective-permute-start(bf16[15,768]{1,0:T(8,128)(2,1)S(1)} %get-tuple-element.35), channel_id=1, source_target_pairs={{0,1},{1,2},{2,3},{3,4},{4,5},{5,6},{6,7},{8,9},{9,10},{10,11},{11... | collective-permute-start | bytes 69128 | tf_op jit(solution)/shard_map/ppermute | solution.py:20
  104.1 67.1 %collective-permute-start.2 = (bf16[15,768]{1,0:T(8,128)(2,1)S(1)}, bf16[15,768]{1,0:T(8,128)(2,1)S(1)}, u32[]{:S(2)}, u32[]{:S(2)}) collective-permute-start(bf16[15,768]{1,0:T(8,128)(2,1)S(1)} %get-tuple-element.36), channel_id=1, source_target_pairs={{1,0},{2,1},{3,2},{4,3},{5,4},{6,5},{7,6},{9,8},{10,9},{11,10},{12... | collective-permute-start | bytes 69128 | tf_op jit(solution)/shard_map/ppermute | solution.py:21
  248.6 5.4 %copy-start.4 = (s32[1,1024]{1,0:T(1,128)S(1)}, s32[1,1024]{1,0:T(1,128)}, u32[]{:S(2)}) copy-start(s32[1,1024]{1,0:T(1,128)} %param.12) | copy-start | bytes 12292
Sparse Core Ops, SparseCore 0:
  10.8 80.9 all-gather.3
  94.5 76.7 all-gather.5
  174.0 74.5 all-gather.7
where the time goes:
time: 291 us
  waiting for transfers between devices  153 us (53%)
  matrix products  71.4 us (25%)
  blocking collectives  26.8 us (9%)
  between operations  16.4 us (6%)
  other arithmetic  9.23 us (3%)
  local copies, waits for them, and re-layouts  8.3 us (3%)
  starting transfers between devices  6 us (2%)
    all_gather x1, waiting for transfers between devices, body(): lax.all_gather(conv_out_weight, ('fsdp', 'seq'), axis=1, tiled=True)  65.5 us
    all_gather x1, waiting for transfers between devices, body(): lax.all_gather(conv_in_weight, ('fsdp', 'seq'), axis=1, tiled=True)  61.1 us
    dot_general x3, matrix products, block_product(): return jnp.dot(left_rows, right_matrix, preferred_element_type=jnp.float32)  60.4 us
    all_gather x1, waiting for transfers between devices, body(): lax.all_gather(head_weight, ('fsdp', 'seq'), axis=1, tiled=True)  25.5 us
    psum x1, blocking collectives, body(): numerator = lax.psum(jnp.sum(frame_error), 'seq')  16.4 us
    psum x1, blocking collectives, body(): frame_error = lax.psum(frame_err, 'seed') / jnp.float32(seed_count)  10.4 us
  transfers between devices with their start and end apart: 6, of which 3 were waited for; matrix products, arithmetic and copies ran while one was open for 28% of the time, Pallas kernels for 0%

commit v1 on v0

--- a/solution.py
+++ b/solution.py
@@ -2,6 +2,18 @@
 import jax.numpy as jnp
 from jax import lax
 from jax.sharding import PartitionSpec as P
+
+
+def unite_members_all_up(matrix, along_dim):
+    return jnp.concatenate(
+        lax.all_to_all(
+            jnp.stack(lax.axis_size(("fsdp", "seq")) * [matrix], 0),
+            axis_name=("fsdp", "seq"),
+            split_axis=0,
+            concat_axis=0,
+        ),
+        axis=along_dim,
+    )
 
 
 def from_behind(x, axis, by):
@@ -91,9 +103,7 @@
     )
     after_conv = stem_out.astype(jnp.float32) + conv_proj
     normed_two = layer_norm(after_conv, gain_rows[1])
-    logits = row_product(
-        normed_two, lax.all_gather(head_weight, ("fsdp", "seq"), axis=1, tiled=True)
-    )
+    logits = row_product(normed_two, unite_members_all_up(head_weight, 1))
     posterior = jax.nn.softmax(logits, axis=-1)
     vocab_size = logits.shape[1]
     onehot = (jnp.arange(vocab_size, dtype=jnp.int32)[None, :] == targets[0][:, None]).astype(

time: 291 us -> 271 us (0.931)
  waiting for transfers between devices: 153 us -> 118 us
  starting transfers between devices: 6 us -> 19.5 us
    all_gather x1 -> x0, waiting for transfers between devices: 25.5 us -> none  [body(): lax.all_gather(head_weight, ('fsdp', 'seq'), axis=1, tiled=True)]
    all_to_all x0 -> x1, starting transfers between devices: none -> 13.6 us  [unite_members_all_up(): lax.all_to_all(jnp.stack(lax.axis_size(('fsdp', 'seq')) * [matrix], 0), a...]
    all_gather x1, waiting for transfers between devices: 61.1 us -> 52 us  [body(): lax.all_gather(conv_in_weight, ('fsdp', 'seq'), axis=1, tiled=True)]
  transfers between devices with their start and end apart: 6 -> 6, of which waited for: 3 -> 2; matrix products, arithmetic and copies ran while one was open for 28% -> 30% of each run, Pallas kernels for 0% -> 0%
where the time goes in v1:
time: 271 us; the launch traced here: 270 us
  waiting for transfers between devices  118 us (44%)
  matrix products  71.3 us (26%)
  blocking collectives  27.1 us (10%)
  starting transfers between devices  19.5 us (7%)
  between operations  16.7 us (6%)
  local copies, waits for them, and re-layouts  9.43 us (3%)
  other arithmetic  7.85 us (3%)
    all_gather x1, waiting for transfers between devices, body(): lax.all_gather(conv_out_weight, ('fsdp', 'seq'), axis=1, tiled=True)  65.5 us
    dot_general x3, matrix products, block_product(): return jnp.dot(left_rows, right_matrix, preferred_element_type=jnp.float32)  60.5 us
    all_gather x1, waiting for transfers between devices, body(): lax.all_gather(conv_in_weight, ('fsdp', 'seq'), axis=1, tiled=True)  52 us
    psum x1, blocking collectives, body(): numerator = lax.psum(jnp.sum(frame_error), 'seq')  16.7 us
    all_to_all x1, starting transfers between devices, unite_members_all_up(): lax.all_to_all(jnp.stack(lax.axis_size(('fsdp', 'seq')) * [matrix], 0), a...  13.6 us
    psum x1, blocking collectives, body(): frame_error = lax.psum(frame_err, 'seed') / jnp.float32(seed_count)  10.4 us
    dot_general x1, matrix products, body(): jnp.dot(blocks, stem_matrix[:half_width], preferred_element_type=jnp.floa...  5.66 us
  transfers between devices with their start and end apart: 6, of which 2 were waited for; matrix products, arithmetic and copies ran while one was open for 30% of the time, Pallas kernels for 0%

profile of v1, /device:TPU:8, one launch (start us, length us, event | category | flops | bytes accessed | tf_op | source)
XLA Modules:
  0.0 270.3 jit_solution(12807974931611391984)
XLA Ops:
  7.2 0.0 copy-start
  7.2 0.0 all-gather.3.cloned.1.call-start
  7.2 0.7 all-gather.3.cloned.1.call-update
  7.9 0.0 all-gather.5.cloned.1.call-start
  8.0 1.5 copy.22
  9.4 0.0 all-gather.5.cloned.1.call-update
  9.5 0.7 slice.261
  10.2 0.1 copy.21
  10.3 0.1 slice.262
  10.4 1.3 collective-permute-start
  11.7 2.0 stack.2
  13.7 0.0 copy-start.3
  13.7 0.0 copy-start.2
  13.7 13.6 %all-to-all-start = ((bf16[64,1,24,512]{3,2,1,0:T(8,128)(2,1)}), bf16[64,1,24,512]{3,2,1,0:T(8,128)(2,1)}, u32[]{:S(2)}, u32[]{:S(2)}) async-start(bf16[64,1,24,512]{3,2,1,0:T(8,128)(2,1)} %stack.2), calls=%async_computation | async-start | bytes 3145728 | tf_op jit(solution)/shard_map/all_to_all | solution.py:9
  27.3 0.0 copy-done
  27.3 0.6 copy.19
  28.0 0.7 reshape_squeeze.3
  29.3 0.0 copy-done.3
  29.4 0.0 copy-done.2
  29.4 0.2 convert_reduce_fusion.31
  29.5 5.7 %fusion.53 = f32[1024,1536]{1,0:T(8,128)} fusion(bf16[1024,320]{1,0:T(8,128)(2,1)S(1)} %reshape_squeeze.3, bf16[1,640,1536]{2,1,0:T(8,128)(2,1)} %param.14), kind=kOutput, calls=%fused_computation.109 | convolution fusion | flops 1006632960 | bytes 7929856 | tf_op jit(solution)/shard_map/dot_general | solution.py:72
  35.2 0.2 slice.259
  35.4 0.6 copy.20
  36.1 1.6 slice.260
  37.7 0.0 collective-permute-done
  37.7 5.2 %convert_reduce_fusion = (f32[1024]{0:T(1024)S(1)}, bf16[1024,1536]{1,0:T(8,128)(2,1)S(1)}) fusion(f32[1024,1536]{1,0:T(8,128)} %fusion.53, bf16[1,640,1536]{2,1,0:T(8,128)(2,1)} %param.14, bf16[1,320]{1,0:T(2,128)(2,1)S(1)} %collective-permute-done, bf16[1023,320]{1,0:T(8,128)(2,1)} %slice.260), kind=kOutput, calls=%fused_computation.2 | convolution fusion | flops 1014234112 | bytes 11211392 | tf_op jit(solution)/shard_map/dot_general | solution.py:73
  42.9 1.0 fusion.2
  43.9 52.0 %all-gather.3.cloned.1.call-done = bf16[1,1536,1536]{2,1,0:T(8,128)(2,1)} async-done(((bf16[1,24,1536]{2,1,0:T(8,128)(2,1)}), bf16[1,1536,1536]{2,1,0:T(8,128)(2,1)}) %all-gather.3.cloned.1.call-update) | async-done | bytes 4718608 | tf_op jit(solution)/shard_map/all_gather | solution.py:85
  95.9 7.2 %fusion.5 = f32[1024,1536]{1,0:T(8,128)S(1)} fusion(bf16[1,1536,1536]{2,1,0:T(8,128)(2,1)} %all-gather.3.cloned.1.call-done, bf16[1024,1536]{1,0:T(8,128)(2,1)S(1)} %get-tuple-element.40, f32[1536]{0:T(1024)S(1)} %get-tuple-element.34, f32[1024]{0:T(1024)S(1)} %add_rsqrt_fusion.1, f32[1024]{0:T(1024)S(1)} %broadcast_multiply_fusion.2), kind=kOutput, calls=%fused_computation.39 | convolution fusion | flops 4839702528 | bytes 14170112 | tf_op jit(solution)/shard_map/dot_general | solution.py:46
  103.2 0.0 copy-start.5
  103.2 0.8 fusion.20
  104.1 0.0 copy-start.1
  104.1 1.1 copy-done.1
  105.2 3.1 %collective-permute-start.1 = (bf16[15,768]{1,0:T(8,128)(2,1)S(1)}, bf16[15,768]{1,0:T(8,128)(2,1)S(1)}, u32[]{:S(2)}, u32[]{:S(2)}) collective-permute-start(bf16[15,768]{1,0:T(8,128)(2,1)S(1)} %get-tuple-element.35), channel_id=1, source_target_pairs={{0,1},{1,2},{2,3},{3,4},{4,5},{5,6},{6,7},{8,9},{9,10},{10,11},{11... | collective-permute-start | bytes 69128 | tf_op jit(solution)/shard_map/ppermute | solution.py:32
  108.3 1.5 collective-permute-start.2
  109.8 0.1 convert_reduce_fusion.30
  109.9 0.0 copy-done.5
  109.9 65.5 %all-gather.5.cloned.1.call-done = bf16[1,768,1536]{2,0,1:T(2,128)(2,1)} async-done(((bf16[1,12,1536]{2,0,1:T(2,128)(2,1)}), bf16[1,768,1536]{2,0,1:T(2,128)(2,1)}) %all-gather.5.cloned.1.call-update) | async-done | bytes 2359312 | tf_op jit(solution)/shard_map/all_gather | solution.py:102
  175.5 0.0 collective-permute-done.1
  175.5 0.0 collective-permute-done.2
  175.5 48.2 %fusion.69 = (f32[1024]{0:T(1024)S(1)}, f32[1024,1536]{1,0:T(8,128)}) fusion(bf16[1,768,1536]{2,0,1:T(2,128)(2,1)} %all-gather.5.cloned.1.call-done, bf16[1024,768]{1,0:T(8,128)(2,1)} %copy-done.1, bf16[15,768]{1,0:T(8,128)(2,1)S(1)} %collective-permute-done.2, bf16[15,768]{1,0:T(8,128)(2,1)S(1)} %collective-permute-done.1, ...), kind=kOutput, calls=%fused_computation.165 | convolution fusion | flops 2567699456 | bytes 13514752 | tf_op jit(solution)/shard_map/dot_general | solution.py:46
  223.7 3.5 %multiply_reduce_fusion = f32[1024]{0:T(1024)S(1)} fusion(f32[1024,1536]{1,0:T(8,128)} %get-tuple-element.42, f32[1024]{0:T(1024)S(1)} %broadcast_multiply_fusion.1), kind=kLoop, calls=%fused_computation.37 | loop fusion | flops 4717568 | bytes 6299648 | tf_op jit(solution)/shard_map/reduce_sum | solution.py:41
  227.2 0.0 all-to-all-done
  227.2 0.0 copy-start.4
  227.3 5.0 %fusion.70 = (f32[1024]{0:T(1024)S(1)}, f32[1024,512]{0,1:T(8,128)S(1)}) fusion(bf16[1536,512]{1,0:T(8,128)(2,1)} %bitcast.5, f32[1024,1536]{1,0:T(8,128)} %get-tuple-element.42, f32[1536]{0:T(1024)S(1)} %get-tuple-element.33, f32[1024]{0:T(1024)S(1)} %add_rsqrt_fusion, f32[1024]{0:T(1024)S(1)} %broadcast_multiply_fusion.1), kind=kOutput, calls=%fused_computation.166 | convolution fusion | flops 1617427456 | bytes 9979904 | tf_op jit(solution)/shard_map/dot_general | solution.py:46
  232.3 0.3 fusion.23
  232.6 0.0 copy-done.4
  232.6 0.7 multiply_reduce_fusion.1
  233.3 10.4 %psum.14 = f32[1024]{0:T(1024)S(1)} all-reduce(f32[1024]{0:T(1024)S(1)} %select_multiply_fusion), channel_id=1, replica_groups=mesh['seed'=4,'fsdp'=8,'seq'=8] {'seed'}, use_global_device_ids=true, to_apply=%region_7.8 | all-reduce | flops 1024 | bytes 8192 | tf_op jit(solution)/shard_map/psum | solution.py:119
  243.7 1.2 fusion.67
  244.9 16.7 %psum.15 = f32[]{:T(128)} all-reduce(f32[]{:T(128)} %get-tuple-element.37), channel_id=1, replica_groups=mesh['seed'=4,'fsdp'=8,'seq'=8] {'seq'}, use_global_device_ids=true, to_apply=%region_9.10 | all-reduce | flops 1 | bytes 8 | tf_op jit(solution)/shard_map/psum | solution.py:120
  (9 shorter events, 0.1 us)
Async XLA Ops:
  7.2 20.1 %copy-start = (bf16[1,4096,80]{1,2,0:T(8,128)(2,1)S(1)}, bf16[1,4096,80]{1,2,0:T(8,128)(2,1)}, u32[]{:S(2)}) copy-start(bf16[1,4096,80]{1,2,0:T(8,128)(2,1)} %param.10) | copy-start | bytes 1966084
  7.2 88.8 %all-gather.3.cloned.1.call-start = ((), (), s32[]{:S(2)}) async-start(), calls=%async_computation.1 | async-start | bytes 4792320 | tf_op jit(solution)/shard_map/all_gather | solution.py:85
  7.9 167.6 %all-gather.5.cloned.1.call-start = ((), (), s32[]{:S(2)}) async-start(), calls=%async_computation.2 | async-start | bytes 4792320 | tf_op jit(solution)/shard_map/all_gather | solution.py:102
  10.4 27.3 %collective-permute-start = (bf16[1,320]{1,0:T(2,128)(2,1)S(1)}, bf16[1,320]{1,0:T(2,128)(2,1)S(1)}, u32[]{:S(2)}, u32[]{:S(2)}) collective-permute-start(bf16[1,320]{1,0:T(2,128)(2,1)S(1)} %slice.262), channel_id=1, source_target_pairs={{1,0},{2,1},{3,2},{4,3},{5,4},{6,5},{7,6},{9,8},{10,9},{11,10},{12... | collective-permute-start | bytes 1928 | tf_op jit(solution)/shard_map/ppermute | solution.py:22
  13.7 15.6 %copy-start.3 = (f32[1,2,1536]{2,1,0:T(2,128)S(1)}, f32[1,2,1536]{2,1,0:T(2,128)}, u32[]{:S(2)}) copy-start(f32[1,2,1536]{2,1,0:T(2,128)} %param.19) | copy-start | bytes 36868
  13.7 15.7 %copy-start.2 = (bf16[1,31,768]{2,1,0:T(8,128)(2,1)S(1)}, bf16[1,31,768]{2,1,0:T(8,128)(2,1)}, u32[]{:S(2)}) copy-start(bf16[1,31,768]{2,1,0:T(8,128)(2,1)} %param.17) | copy-start | bytes 142852
  13.7 213.5 %all-to-all-start = ((bf16[64,1,24,512]{3,2,1,0:T(8,128)(2,1)}), bf16[64,1,24,512]{3,2,1,0:T(8,128)(2,1)}, u32[]{:S(2)}, u32[]{:S(2)}) async-start(bf16[64,1,24,512]{3,2,1,0:T(8,128)(2,1)} %stack.2), calls=%async_computation | async-start | bytes 3145728 | tf_op jit(solution)/shard_map/all_to_all | solution.py:9
  103.2 6.7 %copy-start.5 = (s32[1,1024]{1,0:T(1,128)S(1)}, s32[1,1024]{1,0:T(1,128)}, u32[]{:S(2)}) copy-start(s32[1,1024]{1,0:T(1,128)} %param.13) | copy-start | bytes 12292
  104.1 1.1 copy-start.1
  105.2 70.3 %collective-permute-start.1 = (bf16[15,768]{1,0:T(8,128)(2,1)S(1)}, bf16[15,768]{1,0:T(8,128)(2,1)S(1)}, u32[]{:S(2)}, u32[]{:S(2)}) collective-permute-start(bf16[15,768]{1,0:T(8,128)(2,1)S(1)} %get-tuple-element.35), channel_id=1, source_target_pairs={{0,1},{1,2},{2,3},{3,4},{4,5},{5,6},{6,7},{8,9},{9,10},{10,11},{11... | collective-permute-start | bytes 69128 | tf_op jit(solution)/shard_map/ppermute | solution.py:32
  108.3 67.2 %collective-permute-start.2 = (bf16[15,768]{1,0:T(8,128)(2,1)S(1)}, bf16[15,768]{1,0:T(8,128)(2,1)S(1)}, u32[]{:S(2)}, u32[]{:S(2)}) collective-permute-start(bf16[15,768]{1,0:T(8,128)(2,1)S(1)} %get-tuple-element.36), channel_id=1, source_target_pairs={{1,0},{2,1},{3,2},{4,3},{5,4},{6,5},{7,6},{9,8},{10,9},{11,10},{12... | collective-permute-start | bytes 69128 | tf_op jit(solution)/shard_map/ppermute | solution.py:33
  227.2 5.4 %copy-start.4 = (s32[1,1024]{1,0:T(1,128)S(1)}, s32[1,1024]{1,0:T(1,128)}, u32[]{:S(2)}) copy-start(s32[1,1024]{1,0:T(1,128)} %param.12) | copy-start | bytes 12292
Sparse Core Ops, SparseCore 0:
  10.8 85.1 all-gather.2
  98.7 76.7 all-gather.4
